TPU v7x, 256 devices: a whole 4x4x8 slice. The times are simulated.
256 devices in a mesh: dp: 16 (over x, y_hi, core), tm: 8 (over z), mp: 2 (over y_lo).
Axes of the slice: x: 4, y: 4 (y_hi: 2, y_lo: 2; y = y_hi * 2 + y_lo), z: 8, core: 2. Of those that a mesh axis runs over, the one named last changes fastest.
Arguments:
- query_heads: bfloat16 [16, 16, 256, 2560], P('dp', 'tm', None, 'mp'), may hold values from -4.75 to 4.75
- key_heads: bfloat16 [16, 16, 256, 2560], P('dp', 'tm', None, 'mp'), may hold values from -4.75 to 4.75
- value_heads: bfloat16 [16, 16, 256, 2560], P('dp', 'tm', None, 'mp'), may hold values from -6 to 6
- grad_out: bfloat16 [16, 16, 256, 2560], P('dp', 'tm', None, 'mp'), may hold values from -6 to 6
- out_weight: bfloat16 [2560, 2560], P('dp', 'mp'), may hold values from -0.125 to 0.125
Outputs:
- grad_query: bfloat16 [16, 16, 256, 2560], P('dp', None, 'tm', 'mp')
- grad_key: bfloat16 [16, 16, 256, 2560], P('dp', None, 'tm', 'mp')
- grad_value: bfloat16 [16, 16, 256, 2560], P('dp', None, 'tm', 'mp')
- grad_weight: float32 [2560, 2560], P('dp', 'mp')
All inputs are finite; a program needn't handle non-finite values.
Results may differ from a plain program's by a relative error of at most 0.0058.
Values may be sent and summed in bfloat16 or wider, within the bound.
A program may use at most 128 MiB of HBM per device.

v0:
```python
import jax
import jax.numpy as jnp
from jax import lax
from jax.sharding import PartitionSpec as P

HS = 128


def attend_back(query_part, key_part, value_part, grad_part):
    frame_count = query_part.shape[1]
    score_scale = HS ** (-0.5)
    scores = (
        jnp.einsum("biphs,bjphs->bphij", query_part, key_part, preferred_element_type=jnp.float32)
        * score_scale
    )
    causal = jnp.arange(frame_count)[:, None] >= jnp.arange(frame_count)[None, :]
    scores = jnp.where(causal, scores, jnp.float32(-1e30))
    highest = jnp.max(scores, axis=-1, keepdims=True)
    weights = jnp.exp(scores - highest)
    probs = weights / jnp.sum(weights, axis=-1, keepdims=True)
    probs_low = probs.astype(jnp.bfloat16)
    attended = jnp.einsum(
        "bphij,bjphs->biphs", probs_low, value_part, preferred_element_type=jnp.float32
    ).astype(jnp.bfloat16)
    d_probs = jnp.einsum(
        "biphs,bjphs->bphij", grad_part, value_part, preferred_element_type=jnp.float32
    )
    row_inner = jnp.sum(probs * d_probs, axis=-1, keepdims=True)
    d_scores = (probs * (d_probs - row_inner)).astype(jnp.bfloat16)
    grad_query = (
        jnp.einsum("bphij,bjphs->biphs", d_scores, key_part, preferred_element_type=jnp.float32)
        * score_scale
    ).astype(jnp.bfloat16)
    grad_key = (
        jnp.einsum("bphij,biphs->bjphs", d_scores, query_part, preferred_element_type=jnp.float32)
        * score_scale
    ).astype(jnp.bfloat16)
    grad_value = jnp.einsum(
        "bphij,biphs->bjphs", probs_low, grad_part, preferred_element_type=jnp.float32
    ).astype(jnp.bfloat16)
    return (grad_query, grad_key, grad_value, attended)


def on_device(query_heads, key_heads, value_heads, grad_out, out_weight):
    width = query_heads.shape[3]
    exchanged = (
        lax.all_to_all(query_heads, "tm", split_axis=2, concat_axis=1, tiled=True),
        lax.all_to_all(key_heads, "tm", split_axis=2, concat_axis=1, tiled=True),
        lax.all_to_all(value_heads, "tm", split_axis=2, concat_axis=1, tiled=True),
        lax.all_to_all(grad_out, "tm", split_axis=2, concat_axis=1, tiled=True),
    )
    query_local, key_local, value_local, grad_local = exchanged
    full_grad = lax.all_gather(grad_local, "mp", axis=3, tiled=True)
    batch_local, frame_count, patch_local, out_total = full_grad.shape
    token_rows = full_grad.reshape(-1, out_total)
    columns = token_rows
    d_attended = jnp.dot(
        columns,
        lax.all_gather(out_weight, "dp", axis=0, tiled=True),
        preferred_element_type=jnp.float32,
    ).astype(jnp.bfloat16)
    head_shape = (batch_local, frame_count, patch_local, width // HS, HS)
    grad_query, grad_key, grad_value, attended = attend_back(
        query_local.reshape(head_shape),
        key_local.reshape(head_shape),
        value_local.reshape(head_shape),
        d_attended.reshape(head_shape),
    )
    flat_shape = (batch_local, frame_count, patch_local, width)
    attended_rows = attended.reshape(-1, width)
    token_total = token_rows.shape[0] * lax.axis_size("tm") * lax.axis_size("dp")
    grad_scale = float(token_total) ** (-0.5)
    columns = token_rows
    row_share = lax.psum_scatter(
        lax.dot_general(
            columns, attended_rows, (((0,), (0,)), ((), ())), preferred_element_type=jnp.float32
        ),
        "dp",
        scatter_dimension=0,
        tiled=True,
    )
    grad_weight = lax.psum(row_share, "tm")
    return (
        grad_query.reshape(flat_shape),
        grad_key.reshape(flat_shape),
        grad_value.reshape(flat_shape),
        grad_weight * grad_scale,
    )


def solution(mesh):
    placed = (
        P("dp", "tm", None, "mp"),
        P("dp", "tm", None, "mp"),
        P("dp", "tm", None, "mp"),
        P("dp", "tm", None, "mp"),
        P("dp", "mp"),
    )
    return jax.shard_map(
        on_device,
        mesh=mesh,
        in_specs=placed,
        out_specs=(
            P("dp", None, "tm", "mp"),
            P("dp", None, "tm", "mp"),
            P("dp", None, "tm", "mp"),
            P("dp", "mp"),
        ),
        check_vma=False,
    )
```

profile of v0, /device:TPU:1, one launch (start us, length us, event | category | flops | bytes accessed | tf_op | source)
XLA Modules:
  0.0 419.0 jit_solution(1036720835098711539)
XLA Ops:
  7.2 0.0 all-gather.3.cloned.1.call-start
  7.2 2.7 copy.57
  9.9 41.7 %all_to_all.63 = bf16[1,2,256,1280]{3,1,0,2:T(2,128)(2,1)S(1)} all-to-all(bf16[1,2,256,1280]{3,1,0,2:T(2,128)(2,1)S(1)} %copy.57), channel_id=1, replica_groups=mesh['dp'=16,'tm'=8,'mp'=2] {'tm'}, dimensions={2} | all-to-all | bytes 2621440 | tf_op jit(solution)/shard_map/all_to_all | solution.py:50
  51.5 0.1 copy.58
  51.7 0.0 copy-start.3
  51.7 1.1 copy.59
  52.8 0.0 all-gather.3.cloned.1.call-update
  52.9 0.0 all-gather.5.cloned.1.call-start
  52.9 0.7 all-gather.5.cloned.1.call-update
  53.6 0.0 copy-done.3
  53.6 0.0 copy-start.4
  53.6 2.4 copy.51
  56.0 3.6 all-to-all-start
  59.6 0.0 copy-done.4
  59.6 2.4 copy.53
  62.0 32.3 %all-to-all-done = bf16[1,2,256,1280]{3,1,0,2:T(2,128)(2,1)S(1)} async-done(((bf16[1,2,256,1280]{3,1,0,2:T(2,128)(2,1)}), bf16[1,2,256,1280]{3,1,0,2:T(2,128)(2,1)S(1)}, u32[]{:S(2)}, u32[]{:S(2)}) %all-to-all-start) | async-done | bytes 1310752 | tf_op jit(solution)/shard_map/all_to_all | solution.py:47
  94.3 3.6 all-to-all-start.1
  97.9 3.7 copy.60
  101.6 31.0 %all-to-all-done.1 = bf16[1,2,256,1280]{3,1,0,2:T(2,128)(2,1)S(1)} async-done(((bf16[1,2,256,1280]{3,1,0,2:T(2,128)(2,1)}), bf16[1,2,256,1280]{3,1,0,2:T(2,128)(2,1)S(1)}, u32[]{:S(2)}, u32[]{:S(2)}) %all-to-all-start.1) | async-done | bytes 1310752 | tf_op jit(solution)/shard_map/all_to_all | solution.py:48
  132.6 4.3 %all-to-all-start.3 = ((bf16[1,2,256,1280]{3,1,0,2:T(2,128)(2,1)}), bf16[1,2,256,1280]{3,1,0,2:T(2,128)(2,1)}, u32[]{:S(2)}, u32[]{:S(2)}) async-start(bf16[1,2,256,1280]{3,1,0,2:T(2,128)(2,1)} %copy.60), calls=%async_computation.3 | async-start | bytes 2621440 | tf_op jit(solution)/shard_map/all_to_all | solution.py:49
  136.9 0.2 reduce-scatter.4.cloned.1.call-start
  137.1 1.3 copy.117
  138.4 2.6 reshape.101
  141.0 0.0 copy-start
  141.0 1.4 copy.116
  142.4 3.8 reshape.102
  146.2 25.5 %all-to-all-done.3 = bf16[1,2,256,1280]{3,1,0,2:T(2,128)(2,1)} async-done(((bf16[1,2,256,1280]{3,1,0,2:T(2,128)(2,1)}), bf16[1,2,256,1280]{3,1,0,2:T(2,128)(2,1)}, u32[]{:S(2)}, u32[]{:S(2)}) %all-to-all-start.3) | async-done | bytes 1310752 | tf_op jit(solution)/shard_map/all_to_all | solution.py:49
  171.7 1.5 copy.115
  173.2 1.8 reshape.105
  175.0 0.0 copy-done
  175.0 5.6 %fusion.25 = (f32[32,10,16]{2,1,0:T(8,128)S(1)}, f32[32,10,16,16]{2,3,1,0:T(8,128)}) fusion(pred[16,16]{0,1:T(8,128)(4,1)S(1)} %iota_compare_fusion, bf16[16,32,10,128]{3,2,1,0:T(8,128)(2,1)} %reshape.102, bf16[16,32,10,128]{3,2,1,0:T(8,128)(2,1)S(1)} %reshape.101), kind=kOutput, calls=%fused_computation.41 | convolution fusion | flops 21299216 | bytes 2969856 | tf_op jit(solution)/shard_map/sub | solution.py:19
  180.6 3.4 fusion.2
  184.1 0.5 copy.73
  184.6 0.0 all-gather.3.cloned.1.call-done
  184.6 8.5 %convolution_bitcast_fusion = f32[2560,1280]{0,1:T(8,128)} fusion(bf16[512,2560]{1,0:T(8,128)(2,1)} %bitcast.66, bf16[64,8,10,128]{3,2,1,0:T(8,128)(2,1)S(1)} %bitcast.65), kind=kOutput, calls=%fused_computation.1 | convolution fusion | flops 3355443200 | bytes 17039360 | tf_op jit(solution)/shard_map/dot_general | solution.py:75
  193.1 14.0 %copy.77 = f32[2560,1280]{1,0:T(8,128)} copy(f32[2560,1280]{0,1:T(8,128)} %convolution_bitcast_fusion) | data formatting | bytes 26214400
  207.1 0.0 copy-start.5
  207.1 0.0 reduce-scatter.4.cloned.1.call-update
  207.1 0.0 all-reduce.2.cloned.1.call-start
  207.2 0.0 all-gather.5.cloned.1.call-done
  207.2 1.6 copy-done.5
  208.8 7.5 %convolution_convert_fusion = bf16[512,1280]{1,0:T(8,128)(2,1)} fusion(bf16[512,2560]{1,0:T(8,128)(2,1)S(1)} %bitcast.67, bf16[2560,1280]{1,0:T(8,128)(2,1)} %all-gather.5.cloned.1.call-done), kind=kOutput, calls=%fused_computation.2 | convolution fusion | flops 3356098560 | bytes 10485760 | tf_op jit(solution)/shard_map/dot_general | solution.py:57
  216.3 0.0 copy-start.2
  216.3 4.4 %reshape.104 = bf16[16,32,10,128]{3,2,1,0:T(8,128)(2,1)} reshape(bf16[512,1280]{1,0:T(8,128)(2,1)} %convolution_convert_fusion) | data formatting | bytes 2621440 | tf_op jit(solution)/shard_map/reshape.8
  220.7 0.0 copy-done.2
  220.7 2.9 fusion.3
  223.6 0.5 copy.70
  224.1 1.6 reshape.108
  225.8 7.4 %multiply_reduce_fusion = (f32[32,10,16]{2,1,0:T(8,128)S(1)}, f32[32,10,16,16]{2,3,1,0:T(8,128)}) fusion(f32[32,10,16,16]{2,3,1,0:T(8,128)} %get-tuple-element.21, f32[32,10,16]{2,1,0:T(8,128)S(1)} %get-tuple-element.20, bf16[16,32,10,128]{3,2,1,0:T(8,128)(2,1)} %reshape.105, bf16[16,32,10,128]{3,2,1,0:T(8,128)(2,1)} %reshape.104), kind=kOutput, calls=%fused_computation.6 | convolution fusion | flops 21212160 | bytes 3317760 | tf_op jit(solution)/shard_map/biphs,bjphs->bphij/dot_general | solution.py:25
  233.2 101.9 %reduce-scatter.4.cloned.1.call-done = f32[160,1280]{1,0:T(8,128)} async-done(((f32[2560,1280]{1,0:T(8,128)}), f32[160,1280]{1,0:T(8,128)}) %reduce-scatter.4.cloned.1.call-update) | async-done | bytes 819216
  335.1 2.6 copy.78
  337.7 0.0 all-reduce.2.cloned.1.call-update
  337.7 0.0 copy-start.1
  337.8 3.4 multiply_convert_fusion.2
  341.2 0.0 copy-done.1
  341.2 1.2 fusion.4
  342.3 0.5 copy.66
  342.9 1.6 reshape.106
  344.5 2.6 fusion.5
  347.1 0.5 copy.68
  347.7 1.6 reshape.107
  349.3 60.5 %all-reduce.2.cloned.1.call-done = f32[160,1280]{0,1:T(8,128)} async-done(((f32[160,1280]{0,1:T(8,128)}), f32[160,1280]{0,1:T(8,128)}) %all-reduce.2.cloned.1.call-update) | async-done | bytes 819216 | tf_op jit(solution)/shard_map/psum | solution.py:82
  409.8 1.4 broadcast_multiply_fusion
  411.2 1.3 copy.74
  (1 shorter events, 0.0 us)
Async XLA Ops:
  7.2 177.5 %all-gather.3.cloned.1.call-start = ((), (), s32[]{:S(2)}) async-start(), calls=%async_computation.5 | async-start | bytes 3932160 | tf_op jit(solution)/shard_map/all_gather | solution.py:53
  51.7 1.9 copy-start.3
  52.9 154.3 %all-gather.5.cloned.1.call-start = ((), (), s32[]{:S(2)}) async-start(), calls=%async_computation.6 | async-start | bytes 6963200 | tf_op jit(solution)/shard_map/all_gather | solution.py:59
  53.6 6.0 %copy-start.4 = (bf16[1,2,256,1280]{3,2,1,0:T(8,128)(2,1)S(1)}, bf16[1,2,256,1280]{3,2,1,0:T(8,128)(2,1)}, u32[]{:S(2)}) copy-start(bf16[1,2,256,1280]{3,2,1,0:T(8,128)(2,1)} %param.6) | copy-start | bytes 3932164
  56.0 38.3 %all-to-all-start = ((bf16[1,2,256,1280]{3,1,0,2:T(2,128)(2,1)}), bf16[1,2,256,1280]{3,1,0,2:T(2,128)(2,1)S(1)}, u32[]{:S(2)}, u32[]{:S(2)}) async-start(bf16[1,2,256,1280]{3,1,0,2:T(2,128)(2,1)} %copy.51), calls=%async_computation | async-start | bytes 2621440 | tf_op jit(solution)/shard_map/all_to_all | solution.py:47
  94.3 38.3 %all-to-all-start.1 = ((bf16[1,2,256,1280]{3,1,0,2:T(2,128)(2,1)}), bf16[1,2,256,1280]{3,1,0,2:T(2,128)(2,1)S(1)}, u32[]{:S(2)}, u32[]{:S(2)}) async-start(bf16[1,2,256,1280]{3,1,0,2:T(2,128)(2,1)} %copy.53), calls=%async_computation.1 | async-start | bytes 2621440 | tf_op jit(solution)/shard_map/all_to_all | solution.py:48
  132.6 39.1 %all-to-all-start.3 = ((bf16[1,2,256,1280]{3,1,0,2:T(2,128)(2,1)}), bf16[1,2,256,1280]{3,1,0,2:T(2,128)(2,1)}, u32[]{:S(2)}, u32[]{:S(2)}) async-start(bf16[1,2,256,1280]{3,1,0,2:T(2,128)(2,1)} %copy.60), calls=%async_computation.3 | async-start | bytes 2621440 | tf_op jit(solution)/shard_map/all_to_all | solution.py:49
  136.9 198.2 %reduce-scatter.4.cloned.1.call-start = ((), (), s32[]{:S(2)}) async-start(), calls=%async_computation.8 | async-start | bytes 13926400
  141.0 34.0 %copy-start = (bf16[16,32,10,128]{3,2,1,0:T(8,128)(2,1)}, bf16[16,32,10,128]{3,2,1,0:T(8,128)(2,1)S(1)}, u32[]{:S(2)}) copy-start(bf16[16,32,10,128]{3,2,1,0:T(8,128)(2,1)S(1)} %reshape.101) | copy-start | bytes 3932164
  207.1 1.7 copy-start.5
  207.1 202.7 %all-reduce.2.cloned.1.call-start = ((), (), s32[]{:S(2)}) async-start(), calls=%async_computation.7 | async-start | bytes 2621440 | tf_op jit(solution)/shard_map/psum | solution.py:82
  216.3 4.4 %copy-start.2 = (f32[32,10,16,16]{2,3,1,0:T(8,128)S(1)}, f32[32,10,16,16]{2,3,1,0:T(8,128)}, u32[]{:S(2)}) copy-start(f32[32,10,16,16]{2,3,1,0:T(8,128)} %get-tuple-element.21) | copy-start | bytes 983044
  337.7 3.4 copy-start.1
Sparse Core Ops, SparseCore 0:
  53.0 42.2 all-gather.2
  97.9 71.8 all-gather.4
  207.2 127.8 reduce-scatter.3
  337.9 71.9 all-reduce.1
where the time goes:
time: 424 us; the launch traced here: 419 us
  waiting for transfers between devices  252 us (59%)
  local copies, waits for them, and re-layouts  55.7 us (13%)
  blocking collectives  41.7 us (10%)
  matrix products  39.1 us (9%)
  between operations  14 us (3%)
  starting transfers between devices  11.7 us (3%)
  other arithmetic  4.82 us (1%)
    unnamed x5, waiting for transfers between devices  103 us
    psum x1, waiting for transfers between devices, on_device(): grad_weight = lax.psum(row_share, 'tm')  60.5 us
    all_to_all x1, blocking collectives, on_device(): lax.all_to_all(grad_out, 'tm', split_axis=2, concat_axis=1, tiled=True)  41.7 us
    all_to_all x1, waiting for transfers between devices, on_device(): lax.all_to_all(query_heads, 'tm', split_axis=2, concat_axis=1, tiled=True)  32.3 us
    all_to_all x1, waiting for transfers between devices, on_device(): lax.all_to_all(key_heads, 'tm', split_axis=2, concat_axis=1, tiled=True)  31 us
    unnamed x19, local copies, waits for them, and re-layouts  30.7 us
    all_to_all x1, waiting for transfers between devices, on_device(): lax.all_to_all(value_heads, 'tm', split_axis=2, concat_axis=1, tiled=True)  25.5 us
    another operation x4, local copies, waits for them, and re-layouts  12.6 us
  transfers between devices with their start and end apart: 7, of which 5 were waited for; matrix products, arithmetic and copies ran while one was open for 21% of the time, Pallas kernels for 0%

commit v1 on v0

v1 whole, which is shorter than its diff:
```python
import functools

import jax
import jax.numpy as jnp
from jax import lax
from jax.experimental import pallas as pl
from jax.experimental.pallas import tpu as pltpu
from jax.sharding import PartitionSpec as P

HS = 128
MESH = pl.DeviceIdType.MESH
GROUP = 2
WIDE = GROUP * HS


def kernel(
    dims, query, key, value, grad, weight,
    dq_out, dk_out, dv_out, gw_out,
    G, GT, W, QKV, OUT, DA, ATT, PR, BIAS, CSEND, CRECV, OWN, XSEND, XRECV, ZSEND, ZRECV, ZALL, GW,
    g_send, g_recv, gy_send, gy_recv, w_send, w_recv, wf_send, wf_recv, q_send, q_recv,
    own_g, own_w, own_q, c_send, c_recv, x_send, x_recv, zr_send, zr_recv, za_send, za_recv, out_sem, gw_sem,
):
    groups, grad_scale = dims
    dp, z, m = lax.axis_index("dp"), lax.axis_index("tm"), lax.axis_index("mp")
    c, xh = lax.rem(dp, 2), dp // 2
    sibling = (dp + 1 - 2 * c, z, m)
    partner = (dp, z, 1 - m)

    def z_peer(d):
        return lax.rem(z + d, 8)

    def x_peer(d):
        return lax.rem(xh + d, 8)

    def drain(ref, sem):
        pltpu.make_async_copy(ref, ref, sem).wait()

    def remote(src, dst, ss, rs, to):
        pltpu.make_async_remote_copy(
            src_ref=src, dst_ref=dst, send_sem=ss, recv_sem=rs, device_id=to, device_id_type=MESH
        ).start()

    barrier = pltpu.get_barrier_semaphore()
    for to in [sibling, partner]:
        pl.semaphore_signal(barrier, inc=1, device_id=to, device_id_type=MESH)

    def greet(d, _):
        pl.semaphore_signal(barrier, inc=1, device_id=(dp, z_peer(d), m), device_id_type=MESH)
        pl.semaphore_signal(barrier, inc=1, device_id=(x_peer(d) * 2 + c, z, m), device_id_type=MESH)
        return 0

    lax.fori_loop(1, 8, greet, 0)
    mine = pl.ds(pl.multiple_of(z * 32, 32), 32)
    frames = pl.ds(2 * z, 2)
    pltpu.make_async_copy(grad.at[0, :, mine], G.at[m, frames], own_g).start()
    pltpu.make_async_copy(weight, W.at[xh, c], own_w).start()
    for a, src in enumerate((query, key, value)):
        pltpu.make_async_copy(src.at[0, :, mine], QKV.at[a, frames], own_q).start()
    pl.semaphore_wait(barrier, 16)

    order = (1, 7, 2, 6, 3, 5, 4)

    for i, d in enumerate(order):
        zz = z_peer(d)
        remote(
            grad.at[0, :, pl.ds(pl.multiple_of(zz * 32, 32), 32)], G.at[m, frames], g_send, g_recv.at[i], (dp, zz, m)
        )
    remote(grad.at[0, :, mine], G.at[m, frames], gy_send, gy_recv, partner)

    def send_w(d, _):
        remote(weight, W.at[xh, c], w_send, w_recv, (x_peer(d) * 2 + c, z, m))
        return 0

    lax.fori_loop(1, 8, send_w, 0)

    def send_group(k):
        cols = pl.ds(pl.multiple_of(k * WIDE, WIDE), WIDE)
        for d in order:
            zz = z_peer(d)
            rows = pl.ds(pl.multiple_of(zz * 32, 32), 32)
            for a, src in enumerate((query, key, value)):
                remote(
                    src.at[0, :, rows, cols], QKV.at[a, frames, :, cols], q_send.at[k], q_recv.at[k], (dp, zz, m)
                )

    send_group(0)
    row = lax.broadcasted_iota(jnp.int32, (256, 256), 0)
    col = lax.broadcasted_iota(jnp.int32, (256, 256), 1)
    BIAS[...] = jnp.where((lax.rem(row, 16) == lax.rem(col, 16)) & (col <= row), 0.0, -1e30).astype(jnp.float32)
    ZSEND[:, pl.ds(10 * GROUP, 24 - 10 * GROUP)] = jnp.zeros((groups, 24 - 10 * GROUP, 16, 128), jnp.bfloat16)

    for i, d in enumerate(order):
        zz = lax.rem(z + 8 - d, 8)
        there = G.at[m, pl.ds(2 * zz, 2)]
        drain(there, g_recv.at[i])
        remote(there, there, gy_send, gy_recv, partner)
    send_group(1)
    drain(grad.at[0, :, mine], own_g)

    def turn(half):
        def body(j, _):
            lanes = pl.ds(pl.multiple_of(j * 128, 128), 128)
            block = G[half, :, :, lanes].reshape(512, 128)
            GT[pl.ds(pl.multiple_of(half * 1280 + j * 128, 128), 128), :] = block.T
            return 0

        lax.fori_loop(0, 10, body, 0)

    turn(m)
    drain(W.at[pl.ds(0, 7), c], w_recv)
    drain(weight, own_w)
    remote(W.at[:, c], W.at[:, c], wf_send, wf_recv, sibling)
    drain(G.at[1 - m], gy_recv)
    turn(1 - m)
    drain(W.at[:, 1 - c], wf_recv)
    for a in range(1):
        drain(QKV.at[:, frames], own_q)

    def block_of(ref, b, lanes):
        return ref[:, pl.ds(16 * b, 16), lanes].reshape(256, HS)

    def rows_for(core):
        return jnp.concatenate(
            [GT[pl.ds(pl.multiple_of((2 * s + core) * 160, 32), 160), :] for s in range(8)], axis=0
        )

    def finish_xy(k):
        drain(XRECV.at[k, pl.ds(0, 7)], x_recv.at[k])
        total = XSEND[k, xh].astype(jnp.float32)
        for d in range(1, 8):
            total = total + XRECV[k, x_peer(d)].astype(jnp.float32)
        for h in range(GROUP):
            ZSEND[k, pl.ds(10 * h, 10)] = total[:, h * HS:(h + 1) * HS].astype(jnp.bfloat16).reshape(10, 16, 128)

        def send(d, _):
            zz = z_peer(d)
            remote(ZSEND.at[k, pl.ds(3 * zz, 3)], ZRECV.at[k, z], zr_send.at[k], zr_recv.at[k], (dp, zz, m))
            return 0

        lax.fori_loop(1, 8, send, 0)

    def finish_z(k):
        drain(ZRECV.at[k, pl.ds(0, 7)], zr_recv.at[k])
        total = ZSEND[k, pl.ds(3 * z, 3)].astype(jnp.float32)
        for d in range(1, 8):
            total = total + ZRECV[k, z_peer(d)].astype(jnp.float32)
        ZALL[k, pl.ds(3 * z, 3)] = total.astype(jnp.bfloat16)

        def send(d, _):
            here = ZALL.at[k, pl.ds(3 * z, 3)]
            remote(here, here, za_send.at[k], za_recv.at[k], (dp, z_peer(d), m))
            return 0

        lax.fori_loop(1, 8, send, 0)

    def step(k, _):
        cols = pl.ds(pl.multiple_of(k * WIDE, WIDE), WIDE)
        drain(QKV.at[:, pl.ds(0, 14), :, cols], q_recv.at[k])

        @pl.when(k + 2 < groups)
        def _():
            send_group(k + 2)

        for h in range(GROUP):
            lanes = pl.ds(pl.multiple_of(k * WIDE + h * HS, HS), HS)
            for b in range(2):
                q = block_of(QKV.at[0], b, lanes)
                kk = block_of(QKV.at[1], b, lanes)
                v = block_of(QKV.at[2], b, lanes)
                s = lax.dot_general(q, kk, (((1,), (1,)), ((), ())), preferred_element_type=jnp.float32)
                s = s * (HS ** -0.5) + BIAS[...]
                e = jnp.exp(s - jnp.max(s, axis=-1, keepdims=True))
                p = e / jnp.sum(e, axis=-1, keepdims=True)
                PR[2 * h + b] = p
                att = jnp.dot(p.astype(jnp.bfloat16), v, preferred_element_type=jnp.float32).astype(jnp.bfloat16)
                ATT[:, pl.ds(16 * b, 16), pl.ds(h * HS, HS)] = att.reshape(16, 16, HS)

        att = ATT[...].reshape(512, WIDE)
        theirs = jnp.dot(rows_for(1 - c), att, preferred_element_type=jnp.float32)
        CSEND[k] = theirs.astype(jnp.bfloat16).reshape(8, 160, WIDE)
        remote(CSEND.at[k], CRECV.at[k], c_send.at[k], c_recv.at[k], sibling)
        OWN[...] = jnp.dot(rows_for(c), att, preferred_element_type=jnp.float32).reshape(8, 160, WIDE)

        da = jnp.dot(
            G[0].reshape(512, 1280), W[pl.ds(0, 4), :, :, cols].reshape(1280, WIDE), preferred_element_type=jnp.float32
        )
        da = da + jnp.dot(
            G[1].reshape(512, 1280), W[pl.ds(4, 4), :, :, cols].reshape(1280, WIDE), preferred_element_type=jnp.float32
        )
        DA[...] = da.astype(jnp.bfloat16).reshape(16, 32, WIDE)

        for h in range(GROUP):
            lanes = pl.ds(pl.multiple_of(k * WIDE + h * HS, HS), HS)
            for b in range(2):
                q = block_of(QKV.at[0], b, lanes)
                kk = block_of(QKV.at[1], b, lanes)
                v = block_of(QKV.at[2], b, lanes)
                d_att = block_of(DA, b, pl.ds(h * HS, HS))
                p = PR[2 * h + b]
                dp_ = lax.dot_general(d_att, v, (((1,), (1,)), ((), ())), preferred_element_type=jnp.float32)
                inner = jnp.sum(p * dp_, axis=-1, keepdims=True)
                ds = (p * (dp_ - inner)).astype(jnp.bfloat16)
                over_rows = (((0,), (0,)), ((), ()))
                dq = jnp.dot(ds, kk, preferred_element_type=jnp.float32) * (HS ** -0.5)
                dk = lax.dot_general(ds, q, over_rows, preferred_element_type=jnp.float32) * (HS ** -0.5)
                dv = lax.dot_general(p.astype(jnp.bfloat16), d_att, over_rows, preferred_element_type=jnp.float32)
                for a, r in enumerate((dq, dk, dv)):
                    OUT[a, :, pl.ds(16 * b, 16), lanes] = r.astype(jnp.bfloat16).reshape(16, 16, HS)
        for a, dst in enumerate((dq_out, dk_out, dv_out)):
            pltpu.make_async_copy(OUT.at[a, :, :, cols], dst.at[0, :, :, cols], out_sem).start()

        drain(CRECV.at[k], c_recv.at[k])
        for s in range(8):
            XSEND[k, s] = (OWN[s] + CRECV[k, s].astype(jnp.float32)).astype(jnp.bfloat16)

        def send(d, _):
            to = x_peer(d)
            remote(XSEND.at[k, to], XRECV.at[k, xh], x_send.at[k], x_recv.at[k], (to * 2 + c, z, m))
            return 0

        lax.fori_loop(1, 8, send, 0)

        @pl.when(k >= 1)
        def _():
            finish_xy(k - 1)

        @pl.when(k >= 2)
        def _():
            finish_z(k - 2)

        return 0

    lax.fori_loop(0, groups, step, 0)
    finish_z(groups - 2)
    finish_xy(groups - 1)
    finish_z(groups - 1)

    def place(k, _):
        drain(ZALL.at[k, pl.ds(0, 21)], za_recv.at[k])
        for h in range(GROUP):
            lanes = pl.ds(pl.multiple_of(k * WIDE + h * HS, HS), HS)
            GW[:, lanes] = ZALL[k, pl.ds(10 * h, 10)].astype(jnp.float32).reshape(160, 128) * grad_scale
        return 0

    lax.fori_loop(0, groups, place, 0)
    last = pltpu.make_async_copy(GW, gw_out, gw_sem)
    last.start()

    drain(G.at[m, pl.ds(0, 14)], g_send)
    drain(G.at[m], gy_send)
    drain(W.at[pl.ds(0, 7), c], w_send)
    drain(W.at[:, c], wf_send)

    def settle(k, _):
        cols = pl.ds(pl.multiple_of(k * WIDE, WIDE), WIDE)
        drain(QKV.at[:, pl.ds(0, 14), :, cols], q_send.at[k])
        drain(CSEND.at[k], c_send.at[k])
        drain(XSEND.at[k, pl.ds(0, 7)], x_send.at[k])
        drain(ZRECV.at[k, pl.ds(0, 7)], zr_send.at[k])
        drain(ZALL.at[k, pl.ds(0, 21)], za_send.at[k])
        return 0

    lax.fori_loop(0, groups, settle, 0)
    drain(OUT, out_sem)
    last.wait()


def on_device(query_heads, key_heads, value_heads, grad_out, out_weight):
    groups = query_heads.shape[3] // WIDE
    bf, f32 = jnp.bfloat16, jnp.float32
    dma, vmem = pltpu.SemaphoreType.DMA, pltpu.VMEM
    anywhere = pl.BlockSpec(memory_space=pl.ANY)
    part = jax.ShapeDtypeStruct((1, 16, 32, 1280), bf)
    return pl.pallas_call(
        functools.partial(kernel, (groups, float(16 * 16 * 256) ** -0.5)),
        out_shape=(part, part, part, jax.ShapeDtypeStruct((160, 1280), f32)),
        in_specs=[anywhere] * 5,
        out_specs=(anywhere,) * 4,
        scratch_shapes=[
            vmem((2, 16, 32, 1280), bf),
            vmem((2560, 512), bf),
            vmem((8, 2, 160, 1280), bf),
            vmem((3, 16, 32, 1280), bf),
            vmem((3, 16, 32, 1280), bf),
            vmem((16, 32, WIDE), bf),
            vmem((16, 32, WIDE), bf),
            vmem((2 * GROUP, 256, 256), f32),
            vmem((256, 256), f32),
            vmem((groups, 8, 160, WIDE), bf),
            vmem((groups, 8, 160, WIDE), bf),
            vmem((8, 160, WIDE), f32),
            vmem((groups, 8, 160, WIDE), bf),
            vmem((groups, 8, 160, WIDE), bf),
            vmem((groups, 24, 16, 128), bf),
            vmem((groups, 8, 3, 16, 128), bf),
            vmem((groups, 24, 16, 128), bf),
            vmem((160, 1280), f32),
            dma, dma((7,)), dma, dma, dma, dma, dma, dma, dma((groups,)), dma((groups,)),
            dma, dma, dma, dma((groups,)), dma((groups,)), dma((groups,)), dma((groups,)),
            dma((groups,)), dma((groups,)), dma((groups,)), dma((groups,)), dma, dma,
        ],
        compiler_params=pltpu.CompilerParams(
            collective_id=0, has_side_effects=True, vmem_limit_bytes=58 * 2**20
        ),
    )(query_heads, key_heads, value_heads, grad_out, out_weight)


def solution(mesh):
    placed = (
        P("dp", "tm", None, "mp"),
        P("dp", "tm", None, "mp"),
        P("dp", "tm", None, "mp"),
        P("dp", "tm", None, "mp"),
        P("dp", "mp"),
    )
    return jax.shard_map(
        on_device,
        mesh=mesh,
        in_specs=placed,
        out_specs=(
            P("dp", None, "tm", "mp"),
            P("dp", None, "tm", "mp"),
            P("dp", None, "tm", "mp"),
            P("dp", "mp"),
        ),
        check_vma=False,
    )
```

time: 424 us -> 170 us (0.40)
  waiting for transfers between devices: 252 us -> 0 us
  Pallas kernels: 0 us -> 162 us
  local copies, waits for them, and re-layouts: 55.7 us -> 6.86 us
  blocking collectives: 41.7 us -> 0 us
  matrix products: 39.1 us -> 0 us
  between operations: 14 us -> 0.65 us
  starting transfers between devices: 11.7 us -> 0 us
  other arithmetic: 4.82 us -> 0 us
    pallas_call x0 -> x1, Pallas kernels: none -> 162 us  [on_device(): pl.pallas_call(functools.partial(kernel, (groups, float(16 * 16 * 256) **...]
    unnamed x5 -> x0, waiting for transfers between devices: 103 us -> none
    all_to_all x3 -> x0, waiting for transfers between devices: 88.8 us -> none  [the longest x1 32.3 us: on_device(): lax.all_to_all(query_heads, 'tm', split_axis=2, concat_axis=1, tiled=True)]
    psum x1 -> x0, waiting for transfers between devices: 60.5 us -> none  [on_device(): grad_weight = lax.psum(row_share, 'tm')]
    all_to_all x1 -> x0, blocking collectives: 41.7 us -> none  [on_device(): lax.all_to_all(grad_out, 'tm', split_axis=2, concat_axis=1, tiled=True)]
    dot_general x7 -> x0, matrix products: 33.5 us -> none  [the longest x1 8.48 us: on_device(): lax.dot_general(columns, attended_rows, (((0,), (0,)), ((), ())), preferr...]
    unnamed x19 -> x10, local copies, waits for them, and re-layouts: 30.7 us -> 6.86 us
    another operation x4 -> x0, local copies, waits for them, and re-layouts: 12.6 us -> none
  transfers between devices with their start and end apart: 7 -> 0, of which waited for: 5 -> 0; matrix products, arithmetic and copies ran while one was open for 21% -> 0% of each run, Pallas kernels for 0% -> 0%
where the time goes in v1:
time: 170 us; the launch traced here: 169 us
  Pallas kernels  162 us (95%)
  local copies, waits for them, and re-layouts  6.86 us (4%)
    pallas_call x1, Pallas kernels, on_device(): pl.pallas_call(functools.partial(kernel, (groups, float(16 * 16 * 256) **...  162 us
    unnamed x10, local copies, waits for them, and re-layouts  6.86 us

profile of v1, /device:TPU:1, one launch (start us, length us, event | category | flops | bytes accessed | tf_op | source)
XLA Modules:
  0.0 169.2 jit_solution(18804758593775533)
XLA Ops:
  0.6 161.7 %shard_map.84 = (bf16[1,16,32,1280]{3,2,1,0:T(8,128)(2,1)}, bf16[1,16,32,1280]{3,2,1,0:T(8,128)(2,1)}, bf16[1,16,32,1280]{3,2,1,0:T(8,128)(2,1)}, f32[160,1280]{1,0:T(8,128)}) custom-call(bf16[1,2,256,1280]{3,2,1,0:T(8,128)(2,1)} %query.1, bf16[1,2,256,1280]{3,2,1,0:T(8,128)(2,1)} %key.1, bf16[1,2,256,1280]{3,2,1,0:T(8,128)(2,1)} %value.1, ...), custom_call_target="tpu_custom_call" | custom-call | tf_op jit(solution)/shard_map/pallas_call | solution.py:274
  162.3 0.0 copy-start.1
  162.3 2.6 %copy.13 = bf16[1,16,32,1280]{3,2,1,0:T(8,128)(2,1)} copy(bf16[1,16,32,1280]{3,2,1,0:T(8,128)(2,1)} %get-tuple-element.8) | data formatting | bytes 2621440
  164.9 0.0 copy-done.1
  164.9 0.0 copy-start
  164.9 1.1 copy.14
  166.0 0.7 copy-done
  166.7 0.0 copy-start.2
  166.7 1.1 copy.15
  167.8 0.6 copy-done.2
  168.3 0.9 copy.16
Async XLA Ops:
  162.3 2.6 %copy-start.1 = (bf16[1,16,32,1280]{3,2,1,0:T(8,128)(2,1)S(1)}, bf16[1,16,32,1280]{3,2,1,0:T(8,128)(2,1)}, u32[]{:S(2)}) copy-start(bf16[1,16,32,1280]{3,2,1,0:T(8,128)(2,1)} %get-tuple-element.9) | copy-start | bytes 3932164
  164.9 1.8 %copy-start = (bf16[1,16,32,1280]{3,2,1,0:T(8,128)(2,1)S(1)}, bf16[1,16,32,1280]{3,2,1,0:T(8,128)(2,1)}, u32[]{:S(2)}) copy-start(bf16[1,16,32,1280]{3,2,1,0:T(8,128)(2,1)} %get-tuple-element.10) | copy-start | bytes 3932164
  166.7 1.6 copy-start.2

commit v2 on v1

--- a/solution.py
+++ b/solution.py
@@ -11,14 +11,15 @@
 MESH = pl.DeviceIdType.MESH
 GROUP = 2
 WIDE = GROUP * HS
+OWNED = -(-10 * GROUP // 8)
 
 
 def kernel(
     dims, query, key, value, grad, weight,
-    dq_out, dk_out, dv_out, gw_out,
-    G, GT, W, QKV, OUT, DA, ATT, PR, BIAS, CSEND, CRECV, OWN, XSEND, XRECV, ZSEND, ZRECV, ZALL, GW,
-    g_send, g_recv, gy_send, gy_recv, w_send, w_recv, wf_send, wf_recv, q_send, q_recv,
-    own_g, own_w, own_q, c_send, c_recv, x_send, x_recv, zr_send, zr_recv, za_send, za_recv, out_sem, gw_sem,
+    dq_out, dk_out, dv_out, GW,
+    G, GT, W, QKV, DA, ATT, PR, BIAS, CSEND, CRECV, OWN, XSEND, XRECV, ASEND, ARECV, AALL, BSEND, BRECV, BALL,
+    g_send, g_recv, gy_send, gy_recv, wh_send, wh_recv, w_send, w_recv, wf_send, wf_recv, q_send, q_recv,
+    own_g, own_w, own_q, c_send, c_recv, x_send, x_recv, ar_send, ar_recv, ag_send, ag_recv, br_send, br_recv, bg_send, bg_recv,
 ):
     groups, grad_scale = dims
     dp, z, m = lax.axis_index("dp"), lax.axis_index("tm"), lax.axis_index("mp")
@@ -67,11 +68,14 @@
         )
     remote(grad.at[0, :, mine], G.at[m, frames], gy_send, gy_recv, partner)
 
-    def send_w(d, _):
-        remote(weight, W.at[xh, c], w_send, w_recv, (x_peer(d) * 2 + c, z, m))
-        return 0
-
-    lax.fori_loop(1, 8, send_w, 0)
+    other = xh + 1 - 2 * lax.rem(xh, 2)
+    remote(weight, W.at[xh, c], wh_send, wh_recv, (other * 2 + c, z, m))
+
+    def send_w(src, slot):
+        for d in (2, 6, 4):
+            remote(src, W.at[slot, c], w_send, w_recv, (x_peer(d) * 2 + c, z, m))
+
+    send_w(weight, xh)
 
     def send_group(k):
         cols = pl.ds(pl.multiple_of(k * WIDE, WIDE), WIDE)
@@ -87,13 +91,16 @@
     row = lax.broadcasted_iota(jnp.int32, (256, 256), 0)
     col = lax.broadcasted_iota(jnp.int32, (256, 256), 1)
     BIAS[...] = jnp.where((lax.rem(row, 16) == lax.rem(col, 16)) & (col <= row), 0.0, -1e30).astype(jnp.float32)
-    ZSEND[:, pl.ds(10 * GROUP, 24 - 10 * GROUP)] = jnp.zeros((groups, 24 - 10 * GROUP, 16, 128), jnp.bfloat16)
+    BSEND[...] = jnp.zeros(BSEND.shape, jnp.bfloat16)
 
     for i, d in enumerate(order):
         zz = lax.rem(z + 8 - d, 8)
         there = G.at[m, pl.ds(2 * zz, 2)]
         drain(there, g_recv.at[i])
         remote(there, there, gy_send, gy_recv, partner)
+        if i == 1:
+            drain(weight, wh_recv)
+            send_w(W.at[other, c], other)
     send_group(1)
     drain(grad.at[0, :, mine], own_g)
 
@@ -107,14 +114,12 @@
         lax.fori_loop(0, 10, body, 0)
 
     turn(m)
-    drain(W.at[pl.ds(0, 7), c], w_recv)
+    drain(W.at[pl.ds(0, 6), c], w_recv)
     drain(weight, own_w)
     remote(W.at[:, c], W.at[:, c], wf_send, wf_recv, sibling)
     drain(G.at[1 - m], gy_recv)
     turn(1 - m)
-    drain(W.at[:, 1 - c], wf_recv)
-    for a in range(1):
-        drain(QKV.at[:, frames], own_q)
+    drain(QKV.at[:, frames], own_q)
 
     def block_of(ref, b, lanes):
         return ref[:, pl.ds(16 * b, 16), lanes].reshape(256, HS)
@@ -124,31 +129,30 @@
             [GT[pl.ds(pl.multiple_of((2 * s + core) * 160, 32), 160), :] for s in range(8)], axis=0
         )
 
-    def finish_xy(k):
+    def sum_xy(k):
         drain(XRECV.at[k, pl.ds(0, 7)], x_recv.at[k])
         total = XSEND[k, xh].astype(jnp.float32)
         for d in range(1, 8):
             total = total + XRECV[k, x_peer(d)].astype(jnp.float32)
-        for h in range(GROUP):
-            ZSEND[k, pl.ds(10 * h, 10)] = total[:, h * HS:(h + 1) * HS].astype(jnp.bfloat16).reshape(10, 16, 128)
-
+        return [total[:, h * HS:(h + 1) * HS].astype(jnp.bfloat16) for h in range(GROUP)]
+
+    def scatter_z(src, dst, ss, rs):
         def send(d, _):
             zz = z_peer(d)
-            remote(ZSEND.at[k, pl.ds(3 * zz, 3)], ZRECV.at[k, z], zr_send.at[k], zr_recv.at[k], (dp, zz, m))
+            remote(src.at[zz], dst.at[z], ss, rs, (dp, zz, m))
             return 0
 
         lax.fori_loop(1, 8, send, 0)
 
-    def finish_z(k):
-        drain(ZRECV.at[k, pl.ds(0, 7)], zr_recv.at[k])
-        total = ZSEND[k, pl.ds(3 * z, 3)].astype(jnp.float32)
+    def gather_z(src, dst, all_, rs, ss, gs):
+        drain(dst.at[pl.ds(0, 7)], rs)
+        total = src[z].astype(jnp.float32)
         for d in range(1, 8):
-            total = total + ZRECV[k, z_peer(d)].astype(jnp.float32)
-        ZALL[k, pl.ds(3 * z, 3)] = total.astype(jnp.bfloat16)
+            total = total + dst[z_peer(d)].astype(jnp.float32)
+        all_[z] = total.astype(jnp.bfloat16)
 
         def send(d, _):
-            here = ZALL.at[k, pl.ds(3 * z, 3)]
-            remote(here, here, za_send.at[k], za_recv.at[k], (dp, z_peer(d), m))
+            remote(all_.at[z], all_.at[z], ss, gs, (dp, z_peer(d), m))
             return 0
 
         lax.fori_loop(1, 8, send, 0)
@@ -181,6 +185,19 @@
         remote(CSEND.at[k], CRECV.at[k], c_send.at[k], c_recv.at[k], sibling)
         OWN[...] = jnp.dot(rows_for(c), att, preferred_element_type=jnp.float32).reshape(8, 160, WIDE)
 
+        @pl.when(k >= 1)
+        def _():
+            for h, part in enumerate(sum_xy(k - 1)):
+                ASEND[GROUP * (k - 1) + h] = part
+
+        @pl.when(k == groups - 1)
+        def _():
+            scatter_z(ASEND, ARECV, ar_send, ar_recv)
+
+        @pl.when(k == 0)
+        def _():
+            drain(W.at[:, 1 - c], wf_recv)
+
         da = jnp.dot(
             G[0].reshape(512, 1280), W[pl.ds(0, 4), :, :, cols].reshape(1280, WIDE), preferred_element_type=jnp.float32
         )
@@ -188,6 +205,17 @@
             G[1].reshape(512, 1280), W[pl.ds(4, 4), :, :, cols].reshape(1280, WIDE), preferred_element_type=jnp.float32
         )
         DA[...] = da.astype(jnp.bfloat16).reshape(16, 32, WIDE)
+
+        drain(CRECV.at[k], c_recv.at[k])
+        for s in range(8):
+            XSEND[k, s] = (OWN[s] + CRECV[k, s].astype(jnp.float32)).astype(jnp.bfloat16)
+
+        def send(d, _):
+            to = x_peer(d)
+            remote(XSEND.at[k, to], XRECV.at[k, xh], x_send.at[k], x_recv.at[k], (to * 2 + c, z, m))
+            return 0
+
+        lax.fori_loop(1, 8, send, 0)
 
         for h in range(GROUP):
             lanes = pl.ds(pl.multiple_of(k * WIDE + h * HS, HS), HS)
@@ -204,51 +232,33 @@
                 dq = jnp.dot(ds, kk, preferred_element_type=jnp.float32) * (HS ** -0.5)
                 dk = lax.dot_general(ds, q, over_rows, preferred_element_type=jnp.float32) * (HS ** -0.5)
                 dv = lax.dot_general(p.astype(jnp.bfloat16), d_att, over_rows, preferred_element_type=jnp.float32)
-                for a, r in enumerate((dq, dk, dv)):
-                    OUT[a, :, pl.ds(16 * b, 16), lanes] = r.astype(jnp.bfloat16).reshape(16, 16, HS)
-        for a, dst in enumerate((dq_out, dk_out, dv_out)):
-            pltpu.make_async_copy(OUT.at[a, :, :, cols], dst.at[0, :, :, cols], out_sem).start()
-
-        drain(CRECV.at[k], c_recv.at[k])
-        for s in range(8):
-            XSEND[k, s] = (OWN[s] + CRECV[k, s].astype(jnp.float32)).astype(jnp.bfloat16)
-
-        def send(d, _):
-            to = x_peer(d)
-            remote(XSEND.at[k, to], XRECV.at[k, xh], x_send.at[k], x_recv.at[k], (to * 2 + c, z, m))
-            return 0
-
-        lax.fori_loop(1, 8, send, 0)
-
-        @pl.when(k >= 1)
-        def _():
-            finish_xy(k - 1)
-
-        @pl.when(k >= 2)
-        def _():
-            finish_z(k - 2)
+                for dst, r in ((dq_out, dq), (dk_out, dk), (dv_out, dv)):
+                    dst[0, :, pl.ds(16 * b, 16), lanes] = r.astype(jnp.bfloat16).reshape(16, 16, HS)
 
         return 0
 
     lax.fori_loop(0, groups, step, 0)
-    finish_z(groups - 2)
-    finish_xy(groups - 1)
-    finish_z(groups - 1)
-
-    def place(k, _):
-        drain(ZALL.at[k, pl.ds(0, 21)], za_recv.at[k])
-        for h in range(GROUP):
-            lanes = pl.ds(pl.multiple_of(k * WIDE + h * HS, HS), HS)
-            GW[:, lanes] = ZALL[k, pl.ds(10 * h, 10)].astype(jnp.float32).reshape(160, 128) * grad_scale
-        return 0
-
-    lax.fori_loop(0, groups, place, 0)
-    last = pltpu.make_async_copy(GW, gw_out, gw_sem)
-    last.start()
+    gather_z(ASEND, ARECV, AALL, ar_recv, ag_send, ag_recv)
+    for h, part in enumerate(sum_xy(groups - 1)):
+        for t in range(10):
+            at = 10 * h + t
+            BSEND[at // OWNED, at % OWNED] = part[16 * t:16 * t + 16]
+    scatter_z(BSEND, BRECV, br_send, br_recv)
+    drain(AALL.at[pl.ds(0, 7)], ag_recv)
+    for u in range(8):
+        GW[:, u * HS:(u + 1) * HS] = AALL[u].astype(jnp.float32) * grad_scale
+    gather_z(BSEND, BRECV, BALL, br_recv, bg_send, bg_recv)
+    drain(BALL.at[pl.ds(0, 7)], bg_recv)
+    for h in range(GROUP):
+        for t in range(10):
+            at = 10 * h + t
+            lanes = pl.ds((8 + h) * HS, HS)
+            GW[16 * t:16 * t + 16, lanes] = BALL[at // OWNED, at % OWNED].astype(jnp.float32) * grad_scale
 
     drain(G.at[m, pl.ds(0, 14)], g_send)
     drain(G.at[m], gy_send)
-    drain(W.at[pl.ds(0, 7), c], w_send)
+    drain(weight, wh_send)
+    drain(W.at[pl.ds(0, 6), c], w_send)
     drain(W.at[:, c], wf_send)
 
     def settle(k, _):
@@ -256,31 +266,30 @@
         drain(QKV.at[:, pl.ds(0, 14), :, cols], q_send.at[k])
         drain(CSEND.at[k], c_send.at[k])
         drain(XSEND.at[k, pl.ds(0, 7)], x_send.at[k])
-        drain(ZRECV.at[k, pl.ds(0, 7)], zr_send.at[k])
-        drain(ZALL.at[k, pl.ds(0, 21)], za_send.at[k])
         return 0
 
     lax.fori_loop(0, groups, settle, 0)
-    drain(OUT, out_sem)
-    last.wait()
+    drain(ARECV.at[pl.ds(0, 7)], ar_send)
+    drain(ARECV.at[pl.ds(0, 7)], ag_send)
+    drain(BRECV.at[pl.ds(0, 7)], br_send)
+    drain(BRECV.at[pl.ds(0, 7)], bg_send)
 
 
 def on_device(query_heads, key_heads, value_heads, grad_out, out_weight):
     groups = query_heads.shape[3] // WIDE
     bf, f32 = jnp.bfloat16, jnp.float32
     dma, vmem = pltpu.SemaphoreType.DMA, pltpu.VMEM
-    anywhere = pl.BlockSpec(memory_space=pl.ANY)
+    anywhere = pl.BlockSpec(memory_space=pltpu.HBM)
     part = jax.ShapeDtypeStruct((1, 16, 32, 1280), bf)
     return pl.pallas_call(
         functools.partial(kernel, (groups, float(16 * 16 * 256) ** -0.5)),
         out_shape=(part, part, part, jax.ShapeDtypeStruct((160, 1280), f32)),
         in_specs=[anywhere] * 5,
-        out_specs=(anywhere,) * 4,
+        out_specs=(pl.BlockSpec(memory_space=pltpu.VMEM),) * 4,
         scratch_shapes=[
             vmem((2, 16, 32, 1280), bf),
             vmem((2560, 512), bf),
             vmem((8, 2, 160, 1280), bf),
-            vmem((3, 16, 32, 1280), bf),
             vmem((3, 16, 32, 1280), bf),
             vmem((16, 32, WIDE), bf),
             vmem((16, 32, WIDE), bf),
@@ -291,16 +300,18 @@
             vmem((8, 160, WIDE), f32),
             vmem((groups, 8, 160, WIDE), bf),
             vmem((groups, 8, 160, WIDE), bf),
-            vmem((groups, 24, 16, 128), bf),
-            vmem((groups, 8, 3, 16, 128), bf),
-            vmem((groups, 24, 16, 128), bf),
-            vmem((160, 1280), f32),
-            dma, dma((7,)), dma, dma, dma, dma, dma, dma, dma((groups,)), dma((groups,)),
+            vmem((8, 160, HS), bf),
+            vmem((8, 160, HS), bf),
+            vmem((8, 160, HS), bf),
+            vmem((8, OWNED, 16, HS), bf),
+            vmem((8, OWNED, 16, HS), bf),
+            vmem((8, OWNED, 16, HS), bf),
+            dma, dma((7,)), dma, dma, dma, dma, dma, dma, dma, dma, dma((groups,)), dma((groups,)),
             dma, dma, dma, dma((groups,)), dma((groups,)), dma((groups,)), dma((groups,)),
-            dma((groups,)), dma((groups,)), dma((groups,)), dma((groups,)), dma, dma,
+            dma, dma, dma, dma, dma, dma, dma, dma,
         ],
         compiler_params=pltpu.CompilerParams(
-            collective_id=0, has_side_effects=True, vmem_limit_bytes=58 * 2**20
+            collective_id=0, has_side_effects=True, vmem_limit_bytes=49 * 2**20
         ),
     )(query_heads, key_heads, value_heads, grad_out, out_weight)
 

time: 170 us -> 158 us (0.929)
  Pallas kernels: 162 us -> 151 us
  local copies, waits for them, and re-layouts: 6.86 us -> 5.06 us
    pallas_call x1, Pallas kernels: 162 us -> 151 us  [on_device(): pl.pallas_call(functools.partial(kernel, (groups, float(16 * 16 * 256) **...]
    unnamed x10 -> x6, local copies, waits for them, and re-layouts: 6.86 us -> 5.06 us
where the time goes in v2:
time: 158 us; the launch traced here: 156 us
  Pallas kernels  151 us (96%)
  local copies, waits for them, and re-layouts  5.06 us (3%)
    pallas_call x1, Pallas kernels, on_device(): pl.pallas_call(functools.partial(kernel, (groups, float(16 * 16 * 256) **...  151 us
    unnamed x6, local copies, waits for them, and re-layouts  5.06 us

profile of v2, /device:TPU:1, one launch (start us, length us, event | category | flops | bytes accessed | tf_op | source)
XLA Modules:
  0.0 156.4 jit_solution(15731551645203916665)
XLA Ops:
  0.6 0.0 copy-start
  0.6 1.0 copy-done
  1.6 150.7 %shard_map.84 = (bf16[1,16,32,1280]{3,2,1,0:T(8,128)(2,1)S(1)}, bf16[1,16,32,1280]{3,2,1,0:T(8,128)(2,1)S(1)}, bf16[1,16,32,1280]{3,2,1,0:T(8,128)(2,1)S(1)}, f32[160,1280]{1,0:T(8,128)S(1)}) custom-call(bf16[1,2,256,1280]{3,2,1,0:T(8,128)(2,1)} %query.1, bf16[1,2,256,1280]{3,2,1,0:T(8,128)(2,1)} %key.1, bf16[1,2,256,1280]{3,2,1,0:T(8,128)(2,1)} %value.1, ...), custom_call_target="tpu_custom_call" | custom-call | tf_op jit(solution)/shard_map/pallas_call | solution.py:284
  152.4 1.1 copy.13
  153.4 1.1 copy.14
  154.5 1.1 copy.15
  155.5 0.9 copy.16
Async XLA Ops:
  0.6 1.0 copy-start

commit v3 on v2

--- a/solution.py
+++ b/solution.py
@@ -9,19 +9,17 @@
 
 HS = 128
 MESH = pl.DeviceIdType.MESH
-GROUP = 2
-WIDE = GROUP * HS
-OWNED = -(-10 * GROUP // 8)
+AHEAD = 5
+OWNED = 3
 
 
 def kernel(
-    dims, query, key, value, grad, weight,
+    heads, grad_scale, query, key, value, grad, weight,
     dq_out, dk_out, dv_out, GW,
     G, GT, W, QKV, DA, ATT, PR, BIAS, CSEND, CRECV, OWN, XSEND, XRECV, ASEND, ARECV, AALL, BSEND, BRECV, BALL,
     g_send, g_recv, gy_send, gy_recv, wh_send, wh_recv, w_send, w_recv, wf_send, wf_recv, q_send, q_recv,
     own_g, own_w, own_q, c_send, c_recv, x_send, x_recv, ar_send, ar_recv, ag_send, ag_recv, br_send, br_recv, bg_send, bg_recv,
 ):
-    groups, grad_scale = dims
     dp, z, m = lax.axis_index("dp"), lax.axis_index("tm"), lax.axis_index("mp")
     c, xh = lax.rem(dp, 2), dp // 2
     sibling = (dp + 1 - 2 * c, z, m)
@@ -77,17 +75,21 @@
 
     send_w(weight, xh)
 
-    def send_group(k):
-        cols = pl.ds(pl.multiple_of(k * WIDE, WIDE), WIDE)
+    def columns(u, n):
+        return pl.ds(pl.multiple_of(u * HS, HS), n * HS)
+
+    def send_group(g, u, n):
+        cols = columns(u, n)
         for d in order:
             zz = z_peer(d)
             rows = pl.ds(pl.multiple_of(zz * 32, 32), 32)
             for a, src in enumerate((query, key, value)):
                 remote(
-                    src.at[0, :, rows, cols], QKV.at[a, frames, :, cols], q_send.at[k], q_recv.at[k], (dp, zz, m)
+                    src.at[0, :, rows, cols], QKV.at[a, frames, :, cols], q_send.at[g], q_recv.at[g], (dp, zz, m)
                 )
 
-    send_group(0)
+    send_group(0, 0, 1)
+    send_group(1, 1, 1)
     row = lax.broadcasted_iota(jnp.int32, (256, 256), 0)
     col = lax.broadcasted_iota(jnp.int32, (256, 256), 1)
     BIAS[...] = jnp.where((lax.rem(row, 16) == lax.rem(col, 16)) & (col <= row), 0.0, -1e30).astype(jnp.float32)
@@ -101,7 +103,12 @@
         if i == 1:
             drain(weight, wh_recv)
             send_w(W.at[other, c], other)
-    send_group(1)
+
+    def send_early(g, _):
+        send_group(g, g, 1)
+        return 0
+
+    lax.fori_loop(2, AHEAD, send_early, 0)
     drain(grad.at[0, :, mine], own_g)
 
     def turn(half):
@@ -129,12 +136,13 @@
             [GT[pl.ds(pl.multiple_of((2 * s + core) * 160, 32), 160), :] for s in range(8)], axis=0
         )
 
-    def sum_xy(k):
-        drain(XRECV.at[k, pl.ds(0, 7)], x_recv.at[k])
-        total = XSEND[k, xh].astype(jnp.float32)
-        for d in range(1, 8):
-            total = total + XRECV[k, x_peer(d)].astype(jnp.float32)
-        return [total[:, h * HS:(h + 1) * HS].astype(jnp.bfloat16) for h in range(GROUP)]
+    def sum_xy(g, u, n):
+        drain(XRECV.at[pl.ds(u, n), pl.ds(0, 7)], x_recv.at[g])
+        for h in range(n):
+            total = XSEND[u + h, xh].astype(jnp.float32)
+            for d in range(1, 8):
+                total = total + XRECV[u + h, x_peer(d)].astype(jnp.float32)
+            yield h, total.astype(jnp.bfloat16)
 
     def scatter_z(src, dst, ss, rs):
         def send(d, _):
@@ -157,16 +165,19 @@
 
         lax.fori_loop(1, 8, send, 0)
 
-    def step(k, _):
-        cols = pl.ds(pl.multiple_of(k * WIDE, WIDE), WIDE)
-        drain(QKV.at[:, pl.ds(0, 14), :, cols], q_recv.at[k])
-
-        @pl.when(k + 2 < groups)
-        def _():
-            send_group(k + 2)
-
-        for h in range(GROUP):
-            lanes = pl.ds(pl.multiple_of(k * WIDE + h * HS, HS), HS)
+    def head_rows(k):
+        for _, part in sum_xy(k, k, 1):
+            ASEND[k // 4, pl.ds(2 * lax.rem(k, 4), 2)] = part.reshape(2, 80, HS)
+
+    def head_tiles(g, h):
+        for _, part in sum_xy(g, 8 + h, 1):
+            for t in range(10):
+                at = 10 * h + t
+                BSEND[at // OWNED, at % OWNED] = part[16 * t:16 * t + 16]
+
+    def forward(u, n):
+        for h in range(n):
+            lanes = columns(u + h, 1)
             for b in range(2):
                 q = block_of(QKV.at[0], b, lanes)
                 kk = block_of(QKV.at[1], b, lanes)
@@ -179,46 +190,42 @@
                 att = jnp.dot(p.astype(jnp.bfloat16), v, preferred_element_type=jnp.float32).astype(jnp.bfloat16)
                 ATT[:, pl.ds(16 * b, 16), pl.ds(h * HS, HS)] = att.reshape(16, 16, HS)
 
-        att = ATT[...].reshape(512, WIDE)
-        theirs = jnp.dot(rows_for(1 - c), att, preferred_element_type=jnp.float32)
-        CSEND[k] = theirs.astype(jnp.bfloat16).reshape(8, 160, WIDE)
-        remote(CSEND.at[k], CRECV.at[k], c_send.at[k], c_recv.at[k], sibling)
-        OWN[...] = jnp.dot(rows_for(c), att, preferred_element_type=jnp.float32).reshape(8, 160, WIDE)
-
-        @pl.when(k >= 1)
-        def _():
-            for h, part in enumerate(sum_xy(k - 1)):
-                ASEND[GROUP * (k - 1) + h] = part
-
-        @pl.when(k == groups - 1)
-        def _():
-            scatter_z(ASEND, ARECV, ar_send, ar_recv)
-
-        @pl.when(k == 0)
-        def _():
-            drain(W.at[:, 1 - c], wf_recv)
-
-        da = jnp.dot(
-            G[0].reshape(512, 1280), W[pl.ds(0, 4), :, :, cols].reshape(1280, WIDE), preferred_element_type=jnp.float32
-        )
-        da = da + jnp.dot(
-            G[1].reshape(512, 1280), W[pl.ds(4, 4), :, :, cols].reshape(1280, WIDE), preferred_element_type=jnp.float32
-        )
-        DA[...] = da.astype(jnp.bfloat16).reshape(16, 32, WIDE)
-
-        drain(CRECV.at[k], c_recv.at[k])
-        for s in range(8):
-            XSEND[k, s] = (OWN[s] + CRECV[k, s].astype(jnp.float32)).astype(jnp.bfloat16)
+    def sum_cores(g, u, n):
+        att = ATT[:, :, :n * HS].reshape(512, n * HS)
+        theirs = jnp.dot(rows_for(1 - c), att, preferred_element_type=jnp.float32).astype(jnp.bfloat16)
+        for h in range(n):
+            CSEND[u + h] = theirs[:, h * HS:(h + 1) * HS].reshape(8, 160, HS)
+        part = pl.ds(u, n)
+        remote(CSEND.at[part], CRECV.at[part], c_send.at[g], c_recv.at[g], sibling)
+        own = jnp.dot(rows_for(c), att, preferred_element_type=jnp.float32)
+        for h in range(n):
+            OWN[h] = own[:, h * HS:(h + 1) * HS].reshape(8, 160, HS)
+
+    def to_xy(g, u, n):
+        part = pl.ds(u, n)
+        drain(CRECV.at[part], c_recv.at[g])
+        for h in range(n):
+            for s in range(8):
+                XSEND[u + h, s] = (OWN[h, s] + CRECV[u + h, s].astype(jnp.float32)).astype(jnp.bfloat16)
 
         def send(d, _):
             to = x_peer(d)
-            remote(XSEND.at[k, to], XRECV.at[k, xh], x_send.at[k], x_recv.at[k], (to * 2 + c, z, m))
+            remote(XSEND.at[part, to], XRECV.at[part, xh], x_send.at[g], x_recv.at[g], (to * 2 + c, z, m))
             return 0
 
         lax.fori_loop(1, 8, send, 0)
 
-        for h in range(GROUP):
-            lanes = pl.ds(pl.multiple_of(k * WIDE + h * HS, HS), HS)
+    def d_attended(u, n):
+        cols = columns(u, n)
+        low = W[pl.ds(0, 4), :, :, cols].reshape(1280, n * HS)
+        high = W[pl.ds(4, 4), :, :, cols].reshape(1280, n * HS)
+        da = jnp.dot(G[0].reshape(512, 1280), low, preferred_element_type=jnp.float32)
+        da = da + jnp.dot(G[1].reshape(512, 1280), high, preferred_element_type=jnp.float32)
+        DA[:, :, :n * HS] = da.astype(jnp.bfloat16).reshape(16, 32, n * HS)
+
+    def backward(u, n):
+        for h in range(n):
+            lanes = columns(u + h, 1)
             for b in range(2):
                 q = block_of(QKV.at[0], b, lanes)
                 kk = block_of(QKV.at[1], b, lanes)
@@ -235,21 +242,52 @@
                 for dst, r in ((dq_out, dq), (dk_out, dk), (dv_out, dv)):
                     dst[0, :, pl.ds(16 * b, 16), lanes] = r.astype(jnp.bfloat16).reshape(16, 16, HS)
 
+    def one(k, _):
+        @pl.when(k >= 2)
+        def _():
+            head_rows(k - 2)
+
+        drain(QKV.at[:, pl.ds(0, 14), :, columns(k, 1)], q_recv.at[k])
+
+        @pl.when(k == heads - 1)
+        def _():
+            for i in range(2):
+                scatter_z(ASEND.at[i], ARECV.at[i], ar_send.at[i], ar_recv.at[i])
+
+        @pl.when(k + AHEAD < heads)
+        def _():
+            send_group(k + AHEAD, k + AHEAD, 1)
+
+        forward(k, 1)
+        sum_cores(k, k, 1)
+        to_xy(k, k, 1)
+
+        @pl.when(k == 0)
+        def _():
+            drain(W.at[:, 1 - c], wf_recv)
+
+        d_attended(k, 1)
+        backward(k, 1)
         return 0
 
-    lax.fori_loop(0, groups, step, 0)
-    gather_z(ASEND, ARECV, AALL, ar_recv, ag_send, ag_recv)
-    for h, part in enumerate(sum_xy(groups - 1)):
-        for t in range(10):
-            at = 10 * h + t
-            BSEND[at // OWNED, at % OWNED] = part[16 * t:16 * t + 16]
+    lax.fori_loop(0, heads, one, 0)
+    head_tiles(heads - 2, 0)
+
+    def gather_rows(i):
+        gather_z(ASEND.at[i], ARECV.at[i], AALL.at[i], ar_recv.at[i], ag_send.at[i], ag_recv.at[i])
+
+    gather_rows(0)
+    head_tiles(heads - 1, 1)
     scatter_z(BSEND, BRECV, br_send, br_recv)
-    drain(AALL.at[pl.ds(0, 7)], ag_recv)
-    for u in range(8):
-        GW[:, u * HS:(u + 1) * HS] = AALL[u].astype(jnp.float32) * grad_scale
+    gather_rows(1)
     gather_z(BSEND, BRECV, BALL, br_recv, bg_send, bg_recv)
+    for i in range(2):
+        drain(AALL.at[i, pl.ds(0, 7)], ag_recv.at[i])
+        for u in range(4):
+            rows = AALL[i, 2 * u:2 * u + 2].astype(jnp.float32).reshape(160, HS)
+            GW[:, (4 * i + u) * HS:(4 * i + u + 1) * HS] = rows * grad_scale
     drain(BALL.at[pl.ds(0, 7)], bg_recv)
-    for h in range(GROUP):
+    for h in range(2):
         for t in range(10):
             at = 10 * h + t
             lanes = pl.ds((8 + h) * HS, HS)
@@ -261,28 +299,39 @@
     drain(W.at[pl.ds(0, 6), c], w_send)
     drain(W.at[:, c], wf_send)
 
-    def settle(k, _):
-        cols = pl.ds(pl.multiple_of(k * WIDE, WIDE), WIDE)
-        drain(QKV.at[:, pl.ds(0, 14), :, cols], q_send.at[k])
-        drain(CSEND.at[k], c_send.at[k])
-        drain(XSEND.at[k, pl.ds(0, 7)], x_send.at[k])
+    def settle(g, _):
+        u, n = g, 1
+        drain(QKV.at[:, pl.ds(0, 14), :, columns(u, n)], q_send.at[g])
+        drain(CSEND.at[pl.ds(u, n)], c_send.at[g])
+        drain(XSEND.at[pl.ds(u, n), pl.ds(0, 7)], x_send.at[g])
         return 0
 
-    lax.fori_loop(0, groups, settle, 0)
-    drain(ARECV.at[pl.ds(0, 7)], ar_send)
-    drain(ARECV.at[pl.ds(0, 7)], ag_send)
+    lax.fori_loop(0, heads, settle, 0)
+    for i in range(2):
+        drain(ARECV.at[i, pl.ds(0, 7)], ar_send.at[i])
+        drain(ARECV.at[i, pl.ds(0, 7)], ag_send.at[i])
     drain(BRECV.at[pl.ds(0, 7)], br_send)
     drain(BRECV.at[pl.ds(0, 7)], bg_send)
 
 
+def hand_on(*refs):
+    sems = refs[8]
+    copies = [pltpu.make_async_copy(s, d, sems.at[i]) for i, (s, d) in enumerate(zip(refs[:4], refs[4:8]))]
+    for copy in copies:
+        copy.start()
+    for copy in copies:
+        copy.wait()
+
+
 def on_device(query_heads, key_heads, value_heads, grad_out, out_weight):
-    groups = query_heads.shape[3] // WIDE
+    heads = query_heads.shape[3] // HS
+    groups = heads
     bf, f32 = jnp.bfloat16, jnp.float32
     dma, vmem = pltpu.SemaphoreType.DMA, pltpu.VMEM
     anywhere = pl.BlockSpec(memory_space=pltpu.HBM)
     part = jax.ShapeDtypeStruct((1, 16, 32, 1280), bf)
-    return pl.pallas_call(
-        functools.partial(kernel, (groups, float(16 * 16 * 256) ** -0.5)),
+    results = pl.pallas_call(
+        functools.partial(kernel, heads, float(16 * 16 * 256) ** -0.5),
         out_shape=(part, part, part, jax.ShapeDtypeStruct((160, 1280), f32)),
         in_specs=[anywhere] * 5,
         out_specs=(pl.BlockSpec(memory_space=pltpu.VMEM),) * 4,
@@ -291,29 +340,37 @@
             vmem((2560, 512), bf),
             vmem((8, 2, 160, 1280), bf),
             vmem((3, 16, 32, 1280), bf),
-            vmem((16, 32, WIDE), bf),
-            vmem((16, 32, WIDE), bf),
-            vmem((2 * GROUP, 256, 256), f32),
+            vmem((16, 32, HS), bf),
+            vmem((16, 32, HS), bf),
+            vmem((2, 256, 256), f32),
             vmem((256, 256), f32),
-            vmem((groups, 8, 160, WIDE), bf),
-            vmem((groups, 8, 160, WIDE), bf),
-            vmem((8, 160, WIDE), f32),
-            vmem((groups, 8, 160, WIDE), bf),
-            vmem((groups, 8, 160, WIDE), bf),
-            vmem((8, 160, HS), bf),
-            vmem((8, 160, HS), bf),
-            vmem((8, 160, HS), bf),
+            vmem((heads, 8, 160, HS), bf),
+            vmem((heads, 8, 160, HS), bf),
+            vmem((1, 8, 160, HS), f32),
+            vmem((heads, 8, 160, HS), bf),
+            vmem((heads, 8, 160, HS), bf),
+            vmem((2, 8, 80, HS), bf),
+            vmem((2, 8, 80, HS), bf),
+            vmem((2, 8, 80, HS), bf),
             vmem((8, OWNED, 16, HS), bf),
             vmem((8, OWNED, 16, HS), bf),
             vmem((8, OWNED, 16, HS), bf),
             dma, dma((7,)), dma, dma, dma, dma, dma, dma, dma, dma, dma((groups,)), dma((groups,)),
             dma, dma, dma, dma((groups,)), dma((groups,)), dma((groups,)), dma((groups,)),
-            dma, dma, dma, dma, dma, dma, dma, dma,
+            dma((2,)), dma((2,)), dma((2,)), dma((2,)), dma, dma, dma, dma,
         ],
         compiler_params=pltpu.CompilerParams(
             collective_id=0, has_side_effects=True, vmem_limit_bytes=49 * 2**20
         ),
     )(query_heads, key_heads, value_heads, grad_out, out_weight)
+    return pl.pallas_call(
+        hand_on,
+        out_shape=(part, part, part, jax.ShapeDtypeStruct((160, 1280), f32)),
+        in_specs=[pl.BlockSpec(memory_space=pl.ANY)] * 4,
+        out_specs=(anywhere,) * 4,
+        scratch_shapes=[dma((4,))],
+        compiler_params=pltpu.CompilerParams(vmem_limit_bytes=2**20),
+    )(*results)
 
 
 def solution(mesh):

time: 158 us -> 152 us (0.962)
  local copies, waits for them, and re-layouts: 5.06 us -> 0.99 us
    unnamed x6 -> x2, local copies, waits for them, and re-layouts: 5.06 us -> 0.99 us
    pallas_call x1 -> x2, Pallas kernels: 151 us -> 150 us  [the longest x1 148 us: on_device(): pl.pallas_call(functools.partial(kernel, heads, float(16 * 16 * 256) ** (...]
where the time goes in v3:
time: 152 us
  Pallas kernels  150 us (99%)
    pallas_call x1, Pallas kernels, on_device(): pl.pallas_call(functools.partial(kernel, heads, float(16 * 16 * 256) ** (...  148 us

profile of v3, /device:TPU:1, one launch (start us, length us, event | category | flops | bytes accessed | tf_op | source)
XLA Modules:
  0.0 151.6 jit_solution(4796679536676022060)
XLA Ops:
  0.6 0.0 copy-start
  0.6 1.0 copy-done
  1.6 147.7 %shard_map.84 = (bf16[1,16,32,1280]{3,2,1,0:T(8,128)(2,1)S(1)}, bf16[1,16,32,1280]{3,2,1,0:T(8,128)(2,1)S(1)}, bf16[1,16,32,1280]{3,2,1,0:T(8,128)(2,1)S(1)}, f32[160,1280]{1,0:T(8,128)S(1)}) custom-call(bf16[1,2,256,1280]{3,2,1,0:T(8,128)(2,1)} %query.1, bf16[1,2,256,1280]{3,2,1,0:T(8,128)(2,1)} %key.1, bf16[1,2,256,1280]{3,2,1,0:T(8,128)(2,1)} %value.1, ...), custom_call_target="tpu_custom_call" | custom-call | tf_op jit(solution)/shard_map/pallas_call | solution.py:333
  149.4 2.2 %shard_map.85 = (bf16[1,16,32,1280]{3,2,1,0:T(8,128)(2,1)}, bf16[1,16,32,1280]{3,2,1,0:T(8,128)(2,1)}, bf16[1,16,32,1280]{3,2,1,0:T(8,128)(2,1)}, f32[160,1280]{1,0:T(8,128)}) custom-call(bf16[1,16,32,1280]{3,2,1,0:T(8,128)(2,1)S(1)} %get-tuple-element.8.refs_0_, bf16[1,16,32,1280]{3,2,1,0:T(8,128)(2,1)S(1)} %get-tuple-element.9.refs_1_, ...), custom_call_target="tpu_custom_call" | custom-call | tf_op jit(solution)/shard_map/pallas_call | solution.py:366
Async XLA Ops:
  0.6 1.0 copy-start

commit v4 on v3

--- a/solution.py
+++ b/solution.py
@@ -31,6 +31,9 @@
     def x_peer(d):
         return lax.rem(xh + d, 8)
 
+    def far_first(i):
+        return 4 + ((i + 1) // 2) * (1 - 2 * lax.rem(i, 2))
+
     def drain(ref, sem):
         pltpu.make_async_copy(ref, ref, sem).wait()
 
@@ -57,7 +60,7 @@
         pltpu.make_async_copy(src.at[0, :, mine], QKV.at[a, frames], own_q).start()
     pl.semaphore_wait(barrier, 16)
 
-    order = (1, 7, 2, 6, 3, 5, 4)
+    order = (4, 3, 5, 2, 6, 1, 7)
 
     for i, d in enumerate(order):
         zz = z_peer(d)
@@ -145,12 +148,12 @@
             yield h, total.astype(jnp.bfloat16)
 
     def scatter_z(src, dst, ss, rs):
-        def send(d, _):
-            zz = z_peer(d)
+        def send(i, _):
+            zz = z_peer(far_first(i))
             remote(src.at[zz], dst.at[z], ss, rs, (dp, zz, m))
             return 0
 
-        lax.fori_loop(1, 8, send, 0)
+        lax.fori_loop(0, 7, send, 0)
 
     def gather_z(src, dst, all_, rs, ss, gs):
         drain(dst.at[pl.ds(0, 7)], rs)
@@ -159,11 +162,11 @@
             total = total + dst[z_peer(d)].astype(jnp.float32)
         all_[z] = total.astype(jnp.bfloat16)
 
-        def send(d, _):
-            remote(all_.at[z], all_.at[z], ss, gs, (dp, z_peer(d), m))
+        def send(i, _):
+            remote(all_.at[z], all_.at[z], ss, gs, (dp, z_peer(far_first(i)), m))
             return 0
 
-        lax.fori_loop(1, 8, send, 0)
+        lax.fori_loop(0, 7, send, 0)
 
     def head_rows(k):
         for _, part in sum_xy(k, k, 1):
@@ -208,12 +211,12 @@
             for s in range(8):
                 XSEND[u + h, s] = (OWN[h, s] + CRECV[u + h, s].astype(jnp.float32)).astype(jnp.bfloat16)
 
-        def send(d, _):
-            to = x_peer(d)
+        def send(i, _):
+            to = x_peer(far_first(i))
             remote(XSEND.at[part, to], XRECV.at[part, xh], x_send.at[g], x_recv.at[g], (to * 2 + c, z, m))
             return 0
 
-        lax.fori_loop(1, 8, send, 0)
+        lax.fori_loop(0, 7, send, 0)
 
     def d_attended(u, n):
         cols = columns(u, n)
@@ -316,7 +319,12 @@
 
 def hand_on(*refs):
     sems = refs[8]
-    copies = [pltpu.make_async_copy(s, d, sems.at[i]) for i, (s, d) in enumerate(zip(refs[:4], refs[4:8]))]
+    copies = [
+        pltpu.make_async_copy(s.at[0, pl.ds(8 * i, 8)], d.at[0, pl.ds(8 * i, 8)], sems.at[a, i])
+        for a, (s, d) in enumerate(zip(refs[:3], refs[4:7]))
+        for i in range(2)
+    ]
+    copies.append(pltpu.make_async_copy(refs[3], refs[7], sems.at[3, 0]))
     for copy in copies:
         copy.start()
     for copy in copies:
@@ -368,7 +376,7 @@
         out_shape=(part, part, part, jax.ShapeDtypeStruct((160, 1280), f32)),
         in_specs=[pl.BlockSpec(memory_space=pl.ANY)] * 4,
         out_specs=(anywhere,) * 4,
-        scratch_shapes=[dma((4,))],
+        scratch_shapes=[dma((4, 2))],
         compiler_params=pltpu.CompilerParams(vmem_limit_bytes=2**20),
     )(*results)
 

time: 152 us -> 150 us (0.987)
  no operation moved by 1% of the time
where the time goes in v4:
time: 150 us
  Pallas kernels  149 us (99%)
    pallas_call x1, Pallas kernels, on_device(): pl.pallas_call(functools.partial(kernel, heads, float(16 * 16 * 256) ** (...  146 us

profile of v4, /device:TPU:1, one launch (start us, length us, event | category | flops | bytes accessed | tf_op | source)
XLA Modules:
  0.0 150.4 jit_solution(5941960308517733482)
XLA Ops:
  0.6 0.0 copy-start
  0.6 1.0 copy-done
  1.6 146.5 %shard_map.84 = (bf16[1,16,32,1280]{3,2,1,0:T(8,128)(2,1)S(1)}, bf16[1,16,32,1280]{3,2,1,0:T(8,128)(2,1)S(1)}, bf16[1,16,32,1280]{3,2,1,0:T(8,128)(2,1)S(1)}, f32[160,1280]{1,0:T(8,128)S(1)}) custom-call(bf16[1,2,256,1280]{3,2,1,0:T(8,128)(2,1)} %query.1, bf16[1,2,256,1280]{3,2,1,0:T(8,128)(2,1)} %key.1, bf16[1,2,256,1280]{3,2,1,0:T(8,128)(2,1)} %value.1, ...), custom_call_target="tpu_custom_call" | custom-call | tf_op jit(solution)/shard_map/pallas_call | solution.py:341
  148.1 2.3 %shard_map.85 = (bf16[1,16,32,1280]{3,2,1,0:T(8,128)(2,1)}, bf16[1,16,32,1280]{3,2,1,0:T(8,128)(2,1)}, bf16[1,16,32,1280]{3,2,1,0:T(8,128)(2,1)}, f32[160,1280]{1,0:T(8,128)}) custom-call(bf16[1,16,32,1280]{3,2,1,0:T(8,128)(2,1)S(1)} %get-tuple-element.8.refs_0_, bf16[1,16,32,1280]{3,2,1,0:T(8,128)(2,1)S(1)} %get-tuple-element.9.refs_1_, ...), custom_call_target="tpu_custom_call" | custom-call | tf_op jit(solution)/shard_map/pallas_call | solution.py:374
Async XLA Ops:
  0.6 1.0 copy-start

commit v5 on v4

--- a/solution.py
+++ b/solution.py
@@ -254,8 +254,7 @@
 
         @pl.when(k == heads - 1)
         def _():
-            for i in range(2):
-                scatter_z(ASEND.at[i], ARECV.at[i], ar_send.at[i], ar_recv.at[i])
+            scatter_z(ASEND.at[0], ARECV.at[0], ar_send.at[0], ar_recv.at[0])
 
         @pl.when(k + AHEAD < heads)
         def _():
@@ -264,6 +263,10 @@
         forward(k, 1)
         sum_cores(k, k, 1)
         to_xy(k, k, 1)
+
+        @pl.when(k == heads - 1)
+        def _():
+            scatter_z(ASEND.at[1], ARECV.at[1], ar_send.at[1], ar_recv.at[1])
 
         @pl.when(k == 0)
         def _():

time: 150 us -> 151 us (level)
  no operation moved by 1% of the time
where the time goes in v5:
time: 151 us
  Pallas kernels  149 us (99%)
    pallas_call x1, Pallas kernels, on_device(): pl.pallas_call(functools.partial(kernel, heads, float(16 * 16 * 256) ** (...  147 us

profile of v5, /device:TPU:1, one launch (start us, length us, event | category | flops | bytes accessed | tf_op | source)
XLA Modules:
  0.0 150.6 jit_solution(14945889539882070751)
XLA Ops:
  0.6 0.0 copy-start
  0.6 1.0 copy-done
  1.6 146.7 %shard_map.84 = (bf16[1,16,32,1280]{3,2,1,0:T(8,128)(2,1)S(1)}, bf16[1,16,32,1280]{3,2,1,0:T(8,128)(2,1)S(1)}, bf16[1,16,32,1280]{3,2,1,0:T(8,128)(2,1)S(1)}, f32[160,1280]{1,0:T(8,128)S(1)}) custom-call(bf16[1,2,256,1280]{3,2,1,0:T(8,128)(2,1)} %query.1, bf16[1,2,256,1280]{3,2,1,0:T(8,128)(2,1)} %key.1, bf16[1,2,256,1280]{3,2,1,0:T(8,128)(2,1)} %value.1, ...), custom_call_target="tpu_custom_call" | custom-call | tf_op jit(solution)/shard_map/pallas_call | solution.py:344
  148.4 2.3 %shard_map.85 = (bf16[1,16,32,1280]{3,2,1,0:T(8,128)(2,1)}, bf16[1,16,32,1280]{3,2,1,0:T(8,128)(2,1)}, bf16[1,16,32,1280]{3,2,1,0:T(8,128)(2,1)}, f32[160,1280]{1,0:T(8,128)}) custom-call(bf16[1,16,32,1280]{3,2,1,0:T(8,128)(2,1)S(1)} %get-tuple-element.8.refs_0_, bf16[1,16,32,1280]{3,2,1,0:T(8,128)(2,1)S(1)} %get-tuple-element.9.refs_1_, ...), custom_call_target="tpu_custom_call" | custom-call | tf_op jit(solution)/shard_map/pallas_call | solution.py:377
Async XLA Ops:
  0.6 1.0 copy-start
